TPU v7x, 128 devices: a whole 4x4x4 slice. The times are simulated.
128 devices in a mesh: gx: 8 (over y, core), gy: 16 (over x, z).
Axes of the slice: x: 4, y: 4, z: 4, core: 2. Of those that a mesh axis runs over, the one named last changes fastest.
Arguments:
- outline: float32 [256, 1024, 512], P('gx', 'gy'), may hold values from -0.7 to 0.7, as said below
- centres: float32 [256, 1024, 2], P('gx', 'gy'), may hold values from -0.75 to 0.75
- velocity: float32 [256, 1024, 2], P('gx', 'gy'), may hold values from -6 to 6
- mass: float32 [256, 1024], P('gx', 'gy'), may hold values from 0.5 to 4
- response: float32 [256, 1024, 64], P('gx', 'gy'), may hold values from -0.75 to 0.75
- pairs: int32 [8, 16, 512, 4], P('gx', 'gy'), may hold values from 0 to 2047, as said below
- pair_count: int32 [8, 16], P('gx', 'gy'), may hold values from 1 to 512, as said below
- forcing: float32 [262144, 128], P(('gx', 'gy')), may hold values from -6 to 6
- ocean_dest: int32 [262144, 1], P(('gx', 'gy')), may hold values from 0 to 127; in each aligned block of 2048 rows (0 to 2047, 2048 to 4095, ...) at most 40 rows name the same one
- ocean_floe: int32 [262144], P(('gx', 'gy')), may hold values from 0 to 2047
Outputs:
- final_velocity: float32 [256, 1024, 2], P('gx', 'gy')
- final_centres: float32 [256, 1024, 2], P('gx', 'gy')
Inputs may be any that keep to these rules, and one draw needn't show every extreme that they name: `pairs`: each slot holds a local floe below 2048, a neighbour code below 8, and two tiles below 2; slots from pair_count on are padding. `pair_count`: some block's list is full. `ocean_dest`: the rows of one block name any one block at most 40 times. `outline`: polygon vertices lie at radii 0.3 to 0.7 around the centre, in order of angle.
All inputs are finite; a program needn't handle non-finite values.
Results may differ from a plain program's by a relative error of at most 0.0003.
Values sent between devices are 32-bit elements; how exact they have to be, the bound alone decides.
No kernel may reach another device: no remote copies, remote signals or barrier semaphores. Data moves between devices by JAX's collectives and lax.ppermute only.
A program may use at most 128 MiB of HBM per device.

v0:
```python
import math

import jax
import jax.numpy as jnp
from jax import lax
from jax.sharding import PartitionSpec as P

TILE = 128
STEPS = 3


DIRX = (-1, -1, -1, 0, 0, 1, 1, 1)
DIRY = (-1, 0, 1, -1, 1, -1, 0, 1)
KAPPA = 1.0
INV_WIDTH = 100.0
DT = 0.1
DRAG = 0.5


def with_halo(cells, sides, width):
    for axis, dim in sides:
        count = lax.axis_size(axis)
        ends = count - 1
        head = lax.slice_in_dim(cells, 0, width, axis=dim)
        tail = lax.slice_in_dim(cells, cells.shape[dim] - width, cells.shape[dim], axis=dim)
        cells = jnp.concatenate(
            [
                lax.ppermute(tail, axis, [(i, (i + 1) % count) for i in range(ends)]),
                cells,
                lax.ppermute(head, axis, [((i + 1) % count, i) for i in range(ends)]),
            ],
            axis=dim,
        )
    return cells


def tile_force(own, other, step_x, step_y):
    diff_x = own[:, 0, :, None] - other[:, 0, None, :] - step_x[:, None, None]
    diff_y = own[:, 1, :, None] - other[:, 1, None, :] - step_y[:, None, None]
    weight = jnp.exp(-(diff_x * diff_x + diff_y * diff_y) * INV_WIDTH)
    return KAPPA * jnp.stack(
        [jnp.sum(weight * diff_x, axis=(1, 2)), jnp.sum(weight * diff_y, axis=(1, 2))], axis=1
    )


def table_pick(code, table):
    match = code[:, None] == jnp.arange(8, dtype=jnp.int32)[None, :]
    return jnp.sum(jnp.where(match, jnp.asarray(table, dtype=jnp.int32)[None, :], 0), axis=1)


def tile_terms(rows_table, ntiles, own_idx, own_tile, other_idx, other_tile, step_x, step_y, valid):
    size_b = math.gcd(own_idx.shape[0], 256)
    own_key = own_idx * ntiles + own_tile
    other_key = other_idx * ntiles + other_tile

    def block(items):
        ok_own, ok_other, sx, sy, ok = items
        own = jnp.take(rows_table, ok_own, axis=0)
        other = jnp.take(rows_table, ok_other, axis=0)
        return (
            tile_force(own, other, sx.astype(jnp.float32), sy.astype(jnp.float32))
            * ok.astype(jnp.float32)[:, None]
        )

    def shaped(arr):
        return arr.reshape(-1, size_b)

    return lax.map(
        block, (shaped(own_key), shaped(other_key), shaped(step_x), shaped(step_y), shaped(valid))
    ).reshape(-1, 2)


def contact_forces(extended, pairs, pair_count):
    rows_x = extended.shape[0] - 2
    cols_y = extended.shape[1] - 2
    width = cols_y + 2
    nverts = extended.shape[2] // 2
    ntiles = nverts // TILE
    rows_table = jnp.transpose(extended.reshape(-1, 2, ntiles, TILE), (0, 2, 1, 3)).reshape(
        -1, 2, TILE
    )
    slots = pairs.shape[2]
    lists = pairs[0, 0]
    local = lists[:, 0]
    code = lists[:, 1]
    step_x = table_pick(code, DIRX)
    step_y = table_pick(code, DIRY)
    row = local // cols_y
    col = local % cols_y
    prow = row + step_x
    pcol = col + step_y
    glob_row = lax.axis_index("gx") * rows_x + prow
    glob_col = lax.axis_index("gy") * cols_y + pcol
    inside = (
        (glob_row >= 0)
        & (glob_row < rows_x * lax.axis_size("gx"))
        & (glob_col >= 0)
        & (glob_col < cols_y * lax.axis_size("gy"))
    )
    valid = (jnp.arange(slots, dtype=jnp.int32) < pair_count[0, 0]) & inside
    own_idx = (row + 1) * width + col + 1
    other_idx = (prow + 1) * width + pcol + 1
    forces = tile_terms(
        rows_table, ntiles, own_idx, lists[:, 2], other_idx, lists[:, 3], step_x, step_y, valid
    )
    accum = jnp.zeros(((rows_x + 2) * width, 2), jnp.float32)
    accum = accum.at[own_idx].add(forces).at[other_idx].add(-forces)
    accum = accum.reshape(rows_x + 2, width, 2)
    rim = with_halo(accum, (("gx", 0), ("gy", 1)), 1)
    total = rim[2 : rows_x + 2, 2 : cols_y + 2]
    total = total.at[0].add(rim[0, 2 : cols_y + 2])
    total = total.at[rows_x - 1].add(rim[rows_x + 3, 2 : cols_y + 2])
    total = total.at[:, 0].add(rim[2 : rows_x + 2, 0])
    total = total.at[:, cols_y - 1].add(rim[2 : rows_x + 2, cols_y + 3])
    total = total.at[0, 0].add(rim[0, 0])
    total = total.at[0, cols_y - 1].add(rim[0, cols_y + 3])
    total = total.at[rows_x - 1, 0].add(rim[rows_x + 3, 0])
    total = total.at[rows_x - 1, cols_y - 1].add(rim[rows_x + 3, cols_y + 3])
    return total


def shards(
    outline, centres, velocity, mass, response, pairs, pair_count, forcing, ocean_dest, ocean_floe
):
    rows_x, cols_y, span = outline.shape
    nverts = span // 2
    rows_dev, row_width = forcing.shape
    bins = row_width // 2
    devices = lax.axis_size(("gx", "gy"))
    capacity = max(2, 5 * rows_dev // (2 * devices))
    dest = ocean_dest[:, 0]
    onehot = (dest[:, None] == jnp.arange(devices, dtype=jnp.int32)[None, :]).astype(jnp.int32)
    slot = jnp.sum((jnp.cumsum(onehot, axis=0) - 1) * onehot, axis=1)
    place = dest * capacity + slot
    send_rows = jnp.zeros((devices * capacity, row_width), jnp.float32).at[place].set(forcing)
    send_floe = (
        jnp.zeros((devices * capacity,), jnp.float32).at[place].set(ocean_floe.astype(jnp.float32))
    )
    got_rows, got_floe = (
        lax.all_to_all(
            send_rows.reshape(devices, capacity, row_width),
            ("gx", "gy"),
            split_axis=0,
            concat_axis=0,
            tiled=True,
        ),
        lax.all_to_all(
            send_floe.reshape(devices, capacity),
            ("gx", "gy"),
            split_axis=0,
            concat_axis=0,
            tiled=True,
        ),
    )
    floe_index = got_floe.reshape(-1).astype(jnp.int32)
    ocean_sum = (
        jnp.zeros((rows_x * cols_y, row_width), jnp.float32)
        .at[floe_index]
        .add(got_rows.reshape(-1, row_width))
    )
    ocean_sum = ocean_sum.reshape(rows_x, cols_y, 2, bins)
    ocean_force = jnp.einsum("xycb,xyb->xyc", ocean_sum, response, precision=lax.Precision.HIGHEST)
    shift = centres
    vel = velocity
    for step in range(STEPS):
        positions = outline + jnp.repeat(shift, nverts, axis=2)
        extended = with_halo(positions, (("gx", 0), ("gy", 1)), 1)
        contact = contact_forces(extended, pairs, pair_count)
        vel = vel + DT * (contact + ocean_force - DRAG * vel) / mass[..., None]
        shift = shift + DT * vel
    return (vel, shift)


def solution(mesh):
    return jax.shard_map(
        shards,
        mesh=mesh,
        in_specs=(
            P("gx", "gy", None),
            P("gx", "gy", None),
            P("gx", "gy", None),
            P("gx", "gy"),
            P("gx", "gy", None),
            P("gx", "gy", None, None),
            P("gx", "gy"),
            P(("gx", "gy"), None),
            P(("gx", "gy"), None),
            P(("gx", "gy")),
        ),
        out_specs=(P("gx", "gy", None), P("gx", "gy", None)),
        check_vma=False,
    )
```

profile of v0, /device:TPU:33, one launch (start us, length us, event | category | flops | bytes accessed | tf_op | source)
XLA Modules:
  0.0 517.3 jit_solution(614947783202712078)
XLA Ops:
  5.8 6.5 %reshape.1041 = f32[32,64,512]{2,1,0:T(8,128)} reshape(f32[32,64,2,256]{3,2,1,0:T(2,128)} %broadcast_in_dim.107) | data formatting | bytes 8388608 | tf_op jit(solution)/shard_map/reshape | solution.py:166
  26.2 8.1 %scatter_custom_fusion.2 = f32[5120]{0:T(1024)S(1)} fusion(s32[2048]{0:T(1024)S(1)} %bitcast.256, f32[2048]{0:T(1024)S(1)} %convert_element_type.112, f32[]{:T(128)} %constant.683.clone.1), kind=kCustom, calls=%fused_computation.146 | custom fusion | bytes 20484 | tf_op jit(solution)/shard_map/scatter | solution.py:137
  35.0 10.4 %all-to-all-start = ((f32[128,1,40]{2,1,0:T(1,128)}), f32[128,1,40]{2,1,0:T(1,128)S(1)}, u32[]{:S(2)}, u32[]{:S(2)}) async-start(f32[128,1,40]{2,1,0:T(1,128)} %bitcast.54), calls=%async_computation | async-start | bytes 131072 | tf_op jit(solution)/shard_map/all_to_all | solution.py:147
  47.1 7.5 %scatter_custom_fusion.3 = f32[5120,128]{1,0:T(8,128)} fusion(s32[2048]{0:T(1024)S(1)} %bitcast.257, f32[2048,128]{1,0:T(8,128)} %param.79, f32[]{:T(128)} %constant.683.clone.1), kind=kCustom, calls=%fused_computation.84 | custom fusion | bytes 2621952 | tf_op jit(solution)/shard_map/scatter | solution.py:135
  62.0 21.9 %all-to-all-start.1 = ((f32[128,40,128]{2,1,0:T(8,128)}), f32[128,40,128]{2,1,0:T(8,128)}, u32[]{:S(2)}, u32[]{:S(2)}) async-start(f32[128,40,128]{2,1,0:T(8,128)} %bitcast.199), calls=%async_computation.1 | async-start | bytes 5242880 | tf_op jit(solution)/shard_map/all_to_all | solution.py:140
  88.7 6.5 %reshape.1042 = f32[2244,2,2,128]{3,2,1,0:T(2,128)} reshape(f32[34,66,512]{2,1,0:T(8,128)} %pad_maximum_fusion) | data formatting | bytes 9191424 | tf_op jit(solution)/shard_map/reshape | solution.py:79
  99.0 15.2 %copy.438 = f32[4488,2,128]{2,1,0:T(2,128)} copy(f32[4488,2,128]{2,0,1:T(8,128)S(1)} %bitcast.193) | data formatting | bytes 9191424 | tf_op jit(solution)/shard_map/while | solution.py:68
  114.2 45.6 %while.54 = (s32[]{:T(128)}, f32[2,256,2]{1,2,0:T(2,128)S(1)}, s32[2,256]{1,0:T(2,128)S(1)}, f32[4488,2,128]{2,1,0:T(2,128)}, s32[2,256]{1,0:T(2,128)S(1)}, /*in...) while((s32[]{:T(128)}, f32[2,256,2]{1,2,0:T(2,128)S(1)}, ...), condition=%wide.region_5.7_spmd, body=%wide.region_2.6_spmd.sunk | while | flops 54664960 | bytes 3708269 | solution.py:68
  122.0 15.0 %multiply_reduce_fusion.9 = (f32[256]{0:T(256)S(1)}, f32[256]{0:T(256)S(1)}) fusion(f32[256]{0:T(256)S(1)} %bitcast.246, f32[256,128]{1,0:T(8,128)S(1)} %bitcast.201, f32[256,128]{1,0:T(8,128)S(1)} %bitcast.207, f32[256]{0:T(256)S(1)} %bitcast.245, f32[256,128]{1,0:T(8,128)S(1)} %bitcast.200, f32[256,128]{1,0:T(8,128)S(1)} %bitcast.206), kind=kLoop, calls=%fused_computation.16.clone.1 | loop fusion | flops 54525440 | bytes 528384 | tf_op jit(solution)/shard_map/while/body/eval_jaxpr/reduce_sum | solution.py:42
  144.9 15.0 %multiply_reduce_fusion.9 = (f32[256]{0:T(256)S(1)}, f32[256]{0:T(256)S(1)}) fusion(f32[256]{0:T(256)S(1)} %bitcast.246, f32[256,128]{1,0:T(8,128)S(1)} %bitcast.201, f32[256,128]{1,0:T(8,128)S(1)} %bitcast.207, f32[256]{0:T(256)S(1)} %bitcast.245, f32[256,128]{1,0:T(8,128)S(1)} %bitcast.200, f32[256,128]{1,0:T(8,128)S(1)} %bitcast.206), kind=kLoop, calls=%fused_computation.16.clone.1 | loop fusion | flops 54525440 | bytes 528384 | tf_op jit(solution)/shard_map/while/body/eval_jaxpr/reduce_sum | solution.py:42
  187.6 29.2 %scatter_custom_fusion.4 = f32[2048,128]{1,0:T(8,128)S(1)} fusion(s32[5120]{0:T(1024)S(1)} %bitcast.251, f32[5120,128]{1,0:T(8,128)} %bitcast.57, f32[]{:T(128)} %constant.683.clone.1), kind=kCustom, calls=%fused_computation.100 | custom fusion | flops 655360 | bytes 1049088 | tf_op jit(solution)/shard_map/scatter-add | solution.py:159
  219.3 15.3 %fusion.54 = f32[32,64,1,2]{3,2,1,0:T(1,128)S(1)} fusion(f32[32,64,2,64]{3,2,1,0:T(2,128)} %reshape.1051, f32[32,64,64,1]{2,3,1,0:T(1,128)S(1)} %bitcast.192), kind=kOutput, calls=%fused_computation.203 | convolution fusion | flops 3145728 | bytes 1589248 | tf_op jit(solution)/shard_map/xycb,xyb->xyc/dot_general | solution.py:162
  239.6 6.5 %reshape.1052 = f32[32,64,512]{2,1,0:T(8,128)} reshape(f32[32,64,2,256]{3,2,1,0:T(2,128)} %broadcast_in_dim.114) | data formatting | bytes 8388608 | tf_op jit(solution)/shard_map/reshape | solution.py:166
  278.1 6.5 %reshape.1053 = f32[2244,2,2,128]{3,2,1,0:T(2,128)} reshape(f32[34,66,512]{2,1,0:T(8,128)} %pad_maximum_fusion.1) | data formatting | bytes 9191424 | tf_op jit(solution)/shard_map/reshape | solution.py:79
  288.4 15.2 %copy.456 = f32[4488,2,128]{2,1,0:T(2,128)} copy(f32[4488,2,128]{2,0,1:T(8,128)S(1)} %bitcast.194) | data formatting | bytes 9191424 | tf_op jit(solution)/shard_map/while | solution.py:68
  303.6 45.6 %while.55 = (s32[]{:T(128)}, f32[2,256,2]{1,2,0:T(2,128)S(1)}, s32[2,256]{1,0:T(2,128)S(1)}, f32[4488,2,128]{2,1,0:T(2,128)}, s32[2,256]{1,0:T(2,128)S(1)}, /*in...) while((s32[]{:T(128)}, f32[2,256,2]{1,2,0:T(2,128)S(1)}, ...), condition=%wide.region_20.22_spmd, body=%wide.region_17.21_spmd.sunk | while | flops 54664960 | bytes 3708269 | solution.py:68
  311.4 15.0 %multiply_reduce_fusion.10 = (f32[256]{0:T(256)S(1)}, f32[256]{0:T(256)S(1)}) fusion(f32[256]{0:T(256)S(1)} %bitcast.248, f32[256,128]{1,0:T(8,128)S(1)} %bitcast.203, f32[256,128]{1,0:T(8,128)S(1)} %bitcast.209, f32[256]{0:T(256)S(1)} %bitcast.247, f32[256,128]{1,0:T(8,128)S(1)} %bitcast.202, f32[256,128]{1,0:T(8,128)S(1)} %bitcast.208), kind=kLoop, calls=%fused_computation.38.clone.1 | loop fusion | flops 54525440 | bytes 528384 | tf_op jit(solution)/shard_map/while/body/eval_jaxpr/reduce_sum | solution.py:42
  334.3 15.0 %multiply_reduce_fusion.10 = (f32[256]{0:T(256)S(1)}, f32[256]{0:T(256)S(1)}) fusion(f32[256]{0:T(256)S(1)} %bitcast.248, f32[256,128]{1,0:T(8,128)S(1)} %bitcast.203, f32[256,128]{1,0:T(8,128)S(1)} %bitcast.209, f32[256]{0:T(256)S(1)} %bitcast.247, f32[256,128]{1,0:T(8,128)S(1)} %bitcast.202, f32[256,128]{1,0:T(8,128)S(1)} %bitcast.208), kind=kLoop, calls=%fused_computation.38.clone.1 | loop fusion | flops 54525440 | bytes 528384 | tf_op jit(solution)/shard_map/while/body/eval_jaxpr/reduce_sum | solution.py:42
  381.7 6.5 %reshape.1057 = f32[32,64,512]{2,1,0:T(8,128)} reshape(f32[32,64,2,256]{3,2,1,0:T(2,128)} %broadcast_in_dim.117) | data formatting | bytes 8388608 | tf_op jit(solution)/shard_map/reshape | solution.py:166
  415.9 6.5 %reshape.1058 = f32[2244,2,2,128]{3,2,1,0:T(2,128)} reshape(f32[34,66,512]{2,1,0:T(8,128)} %pad_maximum_fusion.2) | data formatting | bytes 9191424 | tf_op jit(solution)/shard_map/reshape | solution.py:79
  426.2 15.2 %copy.468 = f32[4488,2,128]{2,1,0:T(2,128)} copy(f32[4488,2,128]{2,0,1:T(8,128)S(1)} %bitcast.195) | data formatting | bytes 9191424 | tf_op jit(solution)/shard_map/while | solution.py:68
  441.4 45.6 %while.56 = (s32[]{:T(128)}, f32[2,256,2]{1,2,0:T(2,128)S(1)}, s32[2,256]{1,0:T(2,128)S(1)}, f32[4488,2,128]{2,1,0:T(2,128)}, s32[2,256]{1,0:T(2,128)S(1)}, /*in...) while((s32[]{:T(128)}, f32[2,256,2]{1,2,0:T(2,128)S(1)}, ...), condition=%wide.region_28.30_spmd, body=%wide.region_25.29_spmd.sunk | while | flops 54664960 | bytes 3708269 | solution.py:68
  449.2 15.0 %multiply_reduce_fusion.11 = (f32[256]{0:T(256)S(1)}, f32[256]{0:T(256)S(1)}) fusion(f32[256]{0:T(256)S(1)} %bitcast.250, f32[256,128]{1,0:T(8,128)S(1)} %bitcast.205, f32[256,128]{1,0:T(8,128)S(1)} %bitcast.211, f32[256]{0:T(256)S(1)} %bitcast.249, f32[256,128]{1,0:T(8,128)S(1)} %bitcast.204, f32[256,128]{1,0:T(8,128)S(1)} %bitcast.210), kind=kLoop, calls=%fused_computation.60.clone.1 | loop fusion | flops 54525440 | bytes 528384 | tf_op jit(solution)/shard_map/while/body/eval_jaxpr/reduce_sum | solution.py:42
  472.0 15.0 %multiply_reduce_fusion.11 = (f32[256]{0:T(256)S(1)}, f32[256]{0:T(256)S(1)}) fusion(f32[256]{0:T(256)S(1)} %bitcast.250, f32[256,128]{1,0:T(8,128)S(1)} %bitcast.205, f32[256,128]{1,0:T(8,128)S(1)} %bitcast.211, f32[256]{0:T(256)S(1)} %bitcast.249, f32[256,128]{1,0:T(8,128)S(1)} %bitcast.204, f32[256,128]{1,0:T(8,128)S(1)} %bitcast.210), kind=kLoop, calls=%fused_computation.60.clone.1 | loop fusion | flops 54525440 | bytes 528384 | tf_op jit(solution)/shard_map/while/body/eval_jaxpr/reduce_sum | solution.py:42
  (326 shorter events, 247.3 us)
Async XLA Ops:
  18.8 36.6 %collective-permute-start = (f32[1,64,512]{2,1,0:T(8,128)S(1)}, f32[1,64,512]{2,1,0:T(8,128)S(1)}, u32[]{:S(2)}, u32[]{:S(2)}) collective-permute-start(f32[1,64,512]{2,1,0:T(8,128)S(1)} %get-tuple-element.632), channel_id=1, source_target_pairs={{0,16},{16,32},{32,48},{48,64},{64,80},{80,96},{96,112},{1,17},{17... | collective-permute-start | bytes 393224 | tf_op jit(solution)/shard_map/ppermute | solution.py:28
  22.7 32.7 %collective-permute-start.1 = (f32[1,64,512]{2,1,0:T(8,128)S(1)}, f32[1,64,512]{2,1,0:T(8,128)S(1)}, u32[]{:S(2)}, u32[]{:S(2)}) collective-permute-start(f32[1,64,512]{2,1,0:T(8,128)S(1)} %get-tuple-element.633), channel_id=1, source_target_pairs={{16,0},{32,16},{48,32},{64,48},{80,64},{96,80},{112,96},{17,1},{33... | collective-permute-start | bytes 393224 | tf_op jit(solution)/shard_map/ppermute | solution.py:30
  35.0 27.0 %all-to-all-start = ((f32[128,1,40]{2,1,0:T(1,128)}), f32[128,1,40]{2,1,0:T(1,128)S(1)}, u32[]{:S(2)}, u32[]{:S(2)}) async-start(f32[128,1,40]{2,1,0:T(1,128)} %bitcast.54), calls=%async_computation | async-start | bytes 131072 | tf_op jit(solution)/shard_map/all_to_all | solution.py:147
  56.7 27.5 %collective-permute-start.2 = (f32[34,1,512]{2,0,1:T(8,128)S(1)}, f32[34,1,512]{2,0,1:T(8,128)S(1)}, u32[]{:S(2)}, u32[]{:S(2)}) collective-permute-start(f32[34,1,512]{2,0,1:T(8,128)S(1)} %copy.433), channel_id=1, source_target_pairs={{0,1},{1,2},{2,3},{3,4},{4,5},{5,6},{6,7},{7,8},{8,9},{9,10},{10,1... | collective-permute-start | bytes 208904 | tf_op jit(solution)/shard_map/ppermute | solution.py:28
  60.1 24.2 %collective-permute-start.3 = (f32[34,1,512]{2,0,1:T(8,128)S(1)}, f32[34,1,512]{2,0,1:T(8,128)S(1)}, u32[]{:S(2)}, u32[]{:S(2)}) collective-permute-start(f32[34,1,512]{2,0,1:T(8,128)S(1)} %copy.434), channel_id=1, source_target_pairs={{1,0},{2,1},{3,2},{4,3},{5,4},{6,5},{7,6},{8,7},{9,8},{10,9},{11,1... | collective-permute-start | bytes 208904 | tf_op jit(solution)/shard_map/ppermute | solution.py:30
  62.0 125.6 %all-to-all-start.1 = ((f32[128,40,128]{2,1,0:T(8,128)}), f32[128,40,128]{2,1,0:T(8,128)}, u32[]{:S(2)}, u32[]{:S(2)}) async-start(f32[128,40,128]{2,1,0:T(8,128)} %bitcast.199), calls=%async_computation.1 | async-start | bytes 5242880 | tf_op jit(solution)/shard_map/all_to_all | solution.py:140
  166.8 5.6 %collective-permute-start.4 = (f32[1,66,2]{1,0,2:T(1,128)S(1)}, f32[1,66,2]{1,0,2:T(1,128)S(1)}, u32[]{:S(2)}, u32[]{:S(2)}) collective-permute-start(f32[1,66,2]{1,0,2:T(1,128)S(1)} %bitcast.265), channel_id=1, source_target_pairs={{0,16},{16,32},{32,48},{48,64},{64,80},{80,96},{96,112},{1,17},{17... | collective-permute-start | bytes 1592 | tf_op jit(solution)/shard_map/ppermute | solution.py:28
  175.2 5.5 %collective-permute-start.6 = (f32[36,1,2]{1,0,2:T(8,128)S(1)}, f32[36,1,2]{1,0,2:T(8,128)S(1)}, u32[]{:S(2)}, u32[]{:S(2)}) collective-permute-start(f32[36,1,2]{1,0,2:T(8,128)S(1)} %get-tuple-element.639), channel_id=1, source_target_pairs={{0,1},{1,2},{2,3},{3,4},{4,5},{5,6},{6,7},{7,8},{8,9},{9,10},{10,1... | collective-permute-start | bytes 872 | tf_op jit(solution)/shard_map/ppermute | solution.py:28
  250.6 5.5 %collective-permute-start.8 = (f32[1,64,512]{2,1,0:T(8,128)S(1)}, f32[1,64,512]{2,1,0:T(8,128)S(1)}, u32[]{:S(2)}, u32[]{:S(2)}) collective-permute-start(f32[1,64,512]{2,1,0:T(8,128)S(1)} %get-tuple-element.630), channel_id=1, source_target_pairs={{0,16},{16,32},{32,48},{48,64},{64,80},{80,96},{96,112},{1,17},{17... | collective-permute-start | bytes 393224 | tf_op jit(solution)/shard_map/ppermute | solution.py:28
  254.1 6.3 %collective-permute-start.9 = (f32[1,64,512]{2,1,0:T(8,128)S(1)}, f32[1,64,512]{2,1,0:T(8,128)S(1)}, u32[]{:S(2)}, u32[]{:S(2)}) collective-permute-start(f32[1,64,512]{2,1,0:T(8,128)S(1)} %get-tuple-element.631), channel_id=1, source_target_pairs={{16,0},{32,16},{48,32},{64,48},{80,64},{96,80},{112,96},{17,1},{33... | collective-permute-start | bytes 393224 | tf_op jit(solution)/shard_map/ppermute | solution.py:30
  260.6 7.1 %collective-permute-start.10 = (f32[34,1,512]{2,0,1:T(8,128)S(1)}, f32[34,1,512]{2,0,1:T(8,128)S(1)}, u32[]{:S(2)}, u32[]{:S(2)}) collective-permute-start(f32[34,1,512]{2,0,1:T(8,128)S(1)} %copy.451), channel_id=1, source_target_pairs={{0,1},{1,2},{2,3},{3,4},{4,5},{5,6},{6,7},{7,8},{8,9},{9,10},{10,1... | collective-permute-start | bytes 208904 | tf_op jit(solution)/shard_map/ppermute | solution.py:28
  265.6 8.1 %collective-permute-start.11 = (f32[34,1,512]{2,0,1:T(8,128)S(1)}, f32[34,1,512]{2,0,1:T(8,128)S(1)}, u32[]{:S(2)}, u32[]{:S(2)}) collective-permute-start(f32[34,1,512]{2,0,1:T(8,128)S(1)} %copy.452), channel_id=1, source_target_pairs={{1,0},{2,1},{3,2},{4,3},{5,4},{6,5},{7,6},{8,7},{9,8},{10,9},{11,1... | collective-permute-start | bytes 208904 | tf_op jit(solution)/shard_map/ppermute | solution.py:30
  356.2 5.1 collective-permute-start.12
  359.1 4.9 collective-permute-start.13
  364.1 5.8 %collective-permute-start.14 = (f32[36,1,2]{1,0,2:T(8,128)S(1)}, f32[36,1,2]{1,0,2:T(8,128)S(1)}, u32[]{:S(2)}, u32[]{:S(2)}) collective-permute-start(f32[36,1,2]{1,0,2:T(8,128)S(1)} %get-tuple-element.637), channel_id=1, source_target_pairs={{0,1},{1,2},{2,3},{3,4},{4,5},{5,6},{6,7},{7,8},{8,9},{9,10},{10,1... | collective-permute-start | bytes 872 | tf_op jit(solution)/shard_map/ppermute | solution.py:28
  368.0 5.1 collective-permute-start.15
  392.7 5.0 collective-permute-start.16
  395.8 6.3 %collective-permute-start.17 = (f32[1,64,512]{2,1,0:T(8,128)S(1)}, f32[1,64,512]{2,1,0:T(8,128)S(1)}, u32[]{:S(2)}, u32[]{:S(2)}) collective-permute-start(f32[1,64,512]{2,1,0:T(8,128)S(1)} %get-tuple-element.629), channel_id=1, source_target_pairs={{16,0},{32,16},{48,32},{64,48},{80,64},{96,80},{112,96},{17,1},{33... | collective-permute-start | bytes 393224 | tf_op jit(solution)/shard_map/ppermute | solution.py:30
  402.2 5.8 %collective-permute-start.18 = (f32[34,1,512]{2,0,1:T(8,128)S(1)}, f32[34,1,512]{2,0,1:T(8,128)S(1)}, u32[]{:S(2)}, u32[]{:S(2)}) collective-permute-start(f32[34,1,512]{2,0,1:T(8,128)S(1)} %copy.463), channel_id=1, source_target_pairs={{0,1},{1,2},{2,3},{3,4},{4,5},{5,6},{6,7},{7,8},{8,9},{9,10},{10,1... | collective-permute-start | bytes 208904 | tf_op jit(solution)/shard_map/ppermute | solution.py:28
  405.9 5.6 %collective-permute-start.19 = (f32[34,1,512]{2,0,1:T(8,128)S(1)}, f32[34,1,512]{2,0,1:T(8,128)S(1)}, u32[]{:S(2)}, u32[]{:S(2)}) collective-permute-start(f32[34,1,512]{2,0,1:T(8,128)S(1)} %copy.464), channel_id=1, source_target_pairs={{1,0},{2,1},{3,2},{4,3},{5,4},{6,5},{7,6},{8,7},{9,8},{10,9},{11,1... | collective-permute-start | bytes 208904 | tf_op jit(solution)/shard_map/ppermute | solution.py:30
  494.0 5.5 %collective-permute-start.20 = (f32[1,66,2]{1,0,2:T(1,128)S(1)}, f32[1,66,2]{1,0,2:T(1,128)S(1)}, u32[]{:S(2)}, u32[]{:S(2)}) collective-permute-start(f32[1,66,2]{1,0,2:T(1,128)S(1)} %bitcast.267), channel_id=1, source_target_pairs={{0,16},{16,32},{32,48},{48,64},{64,80},{80,96},{96,112},{1,17},{17... | collective-permute-start | bytes 1592 | tf_op jit(solution)/shard_map/ppermute | solution.py:28
  497.3 4.9 collective-permute-start.21
  502.3 5.5 %collective-permute-start.22 = (f32[36,1,2]{1,0,2:T(8,128)S(1)}, f32[36,1,2]{1,0,2:T(8,128)S(1)}, u32[]{:S(2)}, u32[]{:S(2)}) collective-permute-start(f32[36,1,2]{1,0,2:T(8,128)S(1)} %get-tuple-element.635), channel_id=1, source_target_pairs={{0,1},{1,2},{2,3},{3,4},{4,5},{5,6},{6,7},{7,8},{8,9},{9,10},{10,1... | collective-permute-start | bytes 872 | tf_op jit(solution)/shard_map/ppermute | solution.py:28
  505.9 5.4 %collective-permute-start.23 = (f32[36,1,2]{1,0,2:T(8,128)S(1)}, f32[36,1,2]{1,0,2:T(8,128)S(1)}, u32[]{:S(2)}, u32[]{:S(2)}) collective-permute-start(f32[36,1,2]{1,0,2:T(8,128)S(1)} %get-tuple-element.634), channel_id=1, source_target_pairs={{1,0},{2,1},{3,2},{4,3},{5,4},{6,5},{7,6},{8,7},{9,8},{10,9},{11,1... | collective-permute-start | bytes 872 | tf_op jit(solution)/shard_map/ppermute | solution.py:30
  (16 other events, 463.5 us)
where the time goes:
time: 527 us; the launch traced here: 517 us
  local copies, waits for them, and re-layouts  186 us (35%)
  other arithmetic  179 us (34%)
  starting transfers between devices  98.2 us (19%)
  waiting for transfers between devices  35.1 us (7%)
  matrix products  15.3 us (3%)
    reduce_sum x6, other arithmetic, tile_force(): jnp.sum(weight * diff_x, axis=(1, 2))  89.8 us
    while x3, local copies, waits for them, and re-layouts, tile_terms(): lax.map(block, (shaped(own_key), shaped(other_key), shaped(step_x), shape...  45.6 us
    ppermute x12, starting transfers between devices, with_halo(): lax.ppermute(tail, axis, [(i, (i + 1) % count) for i in range(ends)])  42.5 us
    ppermute x12, waiting for transfers between devices, with_halo(): lax.ppermute(head, axis, [((i + 1) % count, i) for i in range(ends)])  35.1 us
    scatter-add x1, other arithmetic, shards(): ocean_sum = jnp.zeros((rows_x * cols_y, row_width), jnp.float32).at[floe_...  29.2 us
    ppermute x12, starting transfers between devices, with_halo(): lax.ppermute(head, axis, [((i + 1) % count, i) for i in range(ends)])  23.4 us
    all_to_all x1, starting transfers between devices, shards(): lax.all_to_all(send_rows.reshape(devices, capacity, row_width), ('gx', 'g...  21.9 us
    gather x6, local copies, waits for them, and re-layouts, block(): other = jnp.take(rows_table, ok_other, axis=0)  19.8 us
  transfers between devices with their start and end apart: 26, of which 10 were waited for; matrix products, arithmetic and copies ran while one was open for 21% of the time, Pallas kernels for 0%

commit v1 on v0

v1 whole, which is shorter than its diff:
```python
import math

import jax
import jax.numpy as jnp
from jax import lax
from jax.experimental import pallas as pl
from jax.experimental.pallas import tpu as pltpu
from jax.sharding import PartitionSpec as P

FX, FY, V, TILE, NB, PMAX = 32, 64, 256, 128, 64, 512
DEVS, CAP, BLK = 128, 40, 48
STEPS = 3
DT, DRAG = 0.1, 0.5
H = 2
R = FX + 2 * H
NF = R * 128
TW = FY + 16
PADC = 8 - H
NLIST = 9
NCH = NLIST * PMAX // 128
NEIGH = ((0, 0), (-1, 0), (1, 0), (-1, -1), (0, -1), (1, -1), (-1, 1), (0, 1), (1, 1))
SC = math.sqrt(100.0 * math.log2(math.e))
F32, BF16, I32 = jnp.float32, jnp.bfloat16, jnp.int32
VMEM_BYTES = 52 * 1024 * 1024


def params():
    return pltpu.CompilerParams(vmem_limit_bytes=VMEM_BYTES)


def vspec():
    return pl.BlockSpec(memory_space=pltpu.VMEM)


def sspec():
    return pl.BlockSpec(memory_space=pltpu.SMEM)


def aspec():
    return pl.BlockSpec(memory_space=pl.ANY)


def nt(a, b):
    return lax.dot_general(a, b, (((1,), (1,)), ((), ())), preferred_element_type=F32)


def nn(a, b):
    return jnp.dot(a, b, preferred_element_type=F32)


def split3(x):
    a = x.astype(BF16).astype(F32)
    b = (x - a).astype(BF16).astype(F32)
    return a, b, (x - a - b).astype(BF16).astype(F32)


def send_kernel(dest_ref, floe_ref, rows_ref, out_ref, place_v, ids_v, place_s, sem):
    upper = (
        lax.broadcasted_iota(I32, (128, 128), 0) < lax.broadcasted_iota(I32, (128, 128), 1)
    ).astype(F32).astype(BF16)
    ones = jnp.ones((128, 128), BF16)
    index = lax.broadcasted_iota(I32, (128, 128), 0)
    carry = jnp.zeros((128, 128), F32)
    ids = jnp.zeros((128, 128), F32)
    for blk in range(dest_ref.shape[0]):
        dest = dest_ref[blk : blk + 1, :]
        floe = floe_ref[blk : blk + 1, :] + 1
        hot = (index == dest).astype(F32)
        hot16 = hot.astype(BF16)
        rank = jnp.sum(hot * (nn(hot16, upper) + carry), axis=0, keepdims=True)
        carry = carry + nn(hot16, ones)
        rank = rank.astype(I32)
        place_v[blk : blk + 1, :] = dest * BLK + rank
        slot = (index == rank).astype(F32).astype(BF16)
        high = (floe >> 6).astype(F32)
        low = (floe & 63).astype(F32)
        ids = ids + 64.0 * nt((hot * high).astype(BF16), slot) + nt((hot * low).astype(BF16), slot)
    ids_v[...] = ids
    copy = pltpu.make_async_copy(place_v, place_s, sem)
    copy.start()

    @pl.loop(0, out_ref.shape[0] // 128)
    def _(i):
        out_ref[pl.ds(pl.multiple_of(i * 128, 128), 128), :] = jnp.zeros((128, 128), F32)

    copy.wait()

    @pl.loop(0, rows_ref.shape[0] // 16)
    def _(i):
        for j in range(16):
            r = i * 16 + j
            out_ref[pl.ds(place_s[r >> 7, r & 127], 1), :] = rows_ref[pl.ds(r, 1), :]

    @pl.loop(0, DEVS // 8)
    def _(i):
        for j in range(8):
            d = i * 8 + j
            out_ref[pl.ds(d * BLK + CAP, 1), :] = ids_v[pl.ds(d, 1), :]


def ocean_kernel(rows_ref, resp_ref, out_ref, acc_ref, ids_ref):
    groups = rows_ref.shape[0] // 384
    lane = lax.broadcasted_iota(I32, (groups, 128), 1)
    blocks = [jnp.zeros((groups, 128), F32) for _ in range(3)]
    for j in range(8):
        ids = rows_ref[pl.ds(j * BLK + CAP, groups, stride=8 * BLK), :]
        shift = (BLK * j) % 128
        if shift:
            ids = pltpu.roll(ids, shift, 1)
        for b in range(3):
            place = lane + 128 * b - BLK * j
            blocks[b] = jnp.where((place >= 0) & (place < CAP), ids, blocks[b])
    for b in range(3):
        ids_ref[b] = blocks[b]
    acc_ref[...] = jnp.zeros_like(acc_ref)
    base16 = lax.broadcasted_iota(I32, (16, 128), 0).astype(F32)
    one, zero = jnp.ones((16, 128), BF16), jnp.zeros((16, 128), BF16)

    @pl.loop(0, groups)
    def _(g):
        rows = rows_ref[pl.ds(pl.multiple_of(g * 384, 128), 384), :]
        high = rows.astype(BF16)
        low = (rows - high.astype(F32)).astype(BF16)
        both = jnp.concatenate([high, low], axis=1)
        ids = [ids_ref[b, pl.ds(g, 1), :] for b in range(3)]
        for part in range(8):
            cols = []
            for b in range(3):
                rel = jnp.broadcast_to(ids[b] - (part * 256 + 1.0), (16, 128)).astype(BF16)
                cols.append(
                    jnp.concatenate(
                        [jnp.where((base16 + 16.0 * k).astype(BF16) == rel, one, zero) for k in range(16)], axis=0
                    )
                )
            hot = jnp.concatenate(cols, axis=1)
            acc_ref[part * 256 : part * 256 + 256, :] += nn(hot, both)

    out_ref[...] = jnp.zeros_like(out_ref)
    srow = lax.broadcasted_iota(I32, (16, 128), 0)
    slane = lax.broadcasted_iota(I32, (16, 128), 1)
    pick = (((srow == 0) & (slane < NB)) | ((srow == 1) & (slane >= NB))).astype(F32).astype(BF16)
    inner = (slane >= H) & (slane < H + FY)

    @pl.loop(0, 8)
    def _(part):
        at = pl.multiple_of(part * 256, 256)
        total = acc_ref[pl.ds(at, 256), 0:128] + acc_ref[pl.ds(at, 256), 128:256]
        resp = resp_ref[pl.ds(at, 256), :]
        a, b, c = split3(total * jnp.concatenate([resp, resp], axis=1))
        force = nt(pick, a.astype(BF16)) + nt(pick, b.astype(BF16)) + nt(pick, c.astype(BF16))
        for j in range(4):
            piece = force[:, (j // 2) * 128 : (j // 2) * 128 + 128]
            piece = pltpu.roll(piece, (H - 64 * (j % 2)) % 128, 1)
            piece = jnp.where(inner, piece, 0.0)
            out_ref[:, pl.ds(pl.multiple_of((part * 4 + j + H) * 128, 128), 128)] = piece[0:8]


def put_shift(split_ref, sx, sy):
    for k, row in enumerate(split3(sx) + split3(sy)):
        split_ref[k : k + 1, :] = row


def contact_chunk(c, live, words_ref, tiles_ref, split16, hot_ref, b_ref, acc_ref):
    word = words_ref[pl.ds(c, 1), :]
    lane = lax.broadcasted_iota(I32, (1, 128), 1)
    ok = (word >= 0) & (c * 128 + lane < live)
    own = jnp.where(ok, word & 8191, -1)
    other = jnp.where(ok, (word >> 13) & 8191, -1)
    code = (word >> 28) & 7
    code9 = code + (code >= 4).astype(I32)
    step = (code9 >= 3).astype(I32) + (code9 >= 6).astype(I32)
    dirx = (step - 1).astype(F32)
    diry = (code9 - 3 * step - 1).astype(F32)
    index = lax.broadcasted_iota(I32, (128, 128), 0)

    @pl.loop(0, R // 4)
    def _(i):
        for j in range(4):
            r = i * 4 + j
            hot = jnp.where(index == own - r * 128, 1.0, jnp.where(index == other - r * 128, -1.0, 0.0))
            hot_ref[pl.ds(pl.multiple_of(r * 128, 128), 128), :] = hot.astype(BF16)

    hot = hot_ref[...]
    diff = nn(split16, hot)
    dx = (dirx - (diff[0:1] + diff[1:2] + diff[2:3])) * SC
    dy = (diry - (diff[3:4] + diff[4:5] + diff[5:6])) * SC
    px = tiles_ref[c, 2] + dx
    py = tiles_ref[c, 3] + dy
    b_ref[0] = 2.0 * px
    b_ref[1] = 2.0 * py
    b_ref[2] = -(px * px + py * py)
    force_x = jnp.zeros((8, 128), F32)
    force_y = jnp.zeros((8, 128), F32)
    back_x = jnp.zeros((8, 128), F32)
    back_y = jnp.zeros((8, 128), F32)
    for half in range(2):
        ax = [tiles_ref[c, 0, half * 64 + 8 * k : half * 64 + 8 * k + 8, :] for k in range(8)]
        ay = [tiles_ref[c, 1, half * 64 + 8 * k : half * 64 + 8 * k + 8, :] for k in range(8)]
        na = [-(x * x + y * y) for x, y in zip(ax, ay)]

        def body(i, carry):
            sums, bx_sum, by_sum = carry
            sums = list(sums)
            for j in range(4):
                w = i * 4 + j
                bx = jnp.broadcast_to(b_ref[0, pl.ds(w, 1), :], (8, 128))
                by = jnp.broadcast_to(b_ref[1, pl.ds(w, 1), :], (8, 128))
                nb = jnp.broadcast_to(b_ref[2, pl.ds(w, 1), :], (8, 128))
                weights = [jnp.exp2((ax[k] * bx + ay[k] * by) + (na[k] + nb)) for k in range(8)]
                sums = [s + t for s, t in zip(sums, weights)]
                while len(weights) > 1:
                    weights = [weights[k] + weights[k + 1] for k in range(0, len(weights), 2)]
                bx_sum = bx_sum + weights[0] * bx
                by_sum = by_sum + weights[0] * by
            return tuple(sums), bx_sum, by_sum

        sums, back_x, back_y = lax.fori_loop(
            0, TILE // 4, body, (tuple(jnp.zeros((8, 128), F32) for _ in range(8)), back_x, back_y)
        )
        for k in range(8):
            force_x = force_x + ax[k] * sums[k]
            force_y = force_y + ay[k] * sums[k]
    fx = jnp.sum(force_x - 0.5 * back_x, axis=0, keepdims=True) * (1.0 / SC)
    fy = jnp.sum(force_y - 0.5 * back_y, axis=0, keepdims=True) * (1.0 / SC)
    parts = split3(jnp.where(ok, fx, 0.0)) + split3(jnp.where(ok, fy, 0.0))
    srow = lax.broadcasted_iota(I32, (16, 128), 0)
    stacked = jnp.zeros((16, 128), F32)
    for k, row in enumerate(parts):
        stacked = jnp.where(srow == k, jnp.broadcast_to(row, (16, 128)), stacked)
    acc_ref[...] += nt(stacked.astype(BF16), hot)


def chunks(n):
    return (n + 127) >> 7


def acc_rows(acc_ref):
    ax = acc_ref[0:1, :] + acc_ref[1:2, :] + acc_ref[2:3, :]
    ay = acc_ref[3:4, :] + acc_ref[4:5, :] + acc_ref[5:6, :]
    return ax, ay


def first_kernel(
    info_ref, lists_ref, state_ref, outline_ref, north_ref, south_ref, west_ref, east_ref,
    tiles_out, words_out, count_out, force_out,
    table, tiles, stage, raw_v, raw_s, words_s, hot_ref, b_ref, split_ref, acc_ref, sems, tile_sems,
):
    copies = []
    for q in range(4):
        lanes = slice(q * 128, q * 128 + 128)
        for k, (source, target) in enumerate((
            (outline_ref, table.at[q, H : H + FX, 8 : 8 + FY, :]),
            (north_ref, table.at[q, 0:H, 8 : 8 + FY, :]),
            (south_ref, table.at[q, H + FX : R, 8 : 8 + FY, :]),
            (west_ref, table.at[q, :, 0:8, :]),
            (east_ref, table.at[q, :, 8 + FY : 16 + FY, :]),
        )):
            copies.append(pltpu.make_async_copy(source.at[:, :, lanes], target, sems.at[5 * q + k]))
    for copy in copies:
        copy.start()
    row0 = info_ref[0]
    col0 = info_ref[1]
    rows_all = info_ref[2]
    cols_all = info_ref[3]
    slot = lax.broadcasted_iota(I32, (1, PMAX), 1)
    for k, (di, dj) in enumerate(NEIGH):
        local = lists_ref[4 * k : 4 * k + 1, :].astype(I32)
        code = lists_ref[4 * k + 1 : 4 * k + 2, :].astype(I32)
        mine = lists_ref[4 * k + 2 : 4 * k + 3, :].astype(I32)
        theirs = lists_ref[4 * k + 3 : 4 * k + 4, :].astype(I32)
        code9 = code + (code >= 4).astype(I32)
        step = (code9 >= 3).astype(I32) + (code9 >= 6).astype(I32)
        row = (local >> 6) + di * FX
        col = (local & 63) + dj * FY
        prow = row + step - 1
        pcol = col + code9 - 3 * step - 1
        ok = (slot < info_ref[4 + k]) & (prow + row0 >= 0) & (prow + row0 < rows_all)
        ok = ok & (pcol + col0 >= 0) & (pcol + col0 < cols_all)
        if k:
            near = (row >= -1) & (row <= FX) & (col >= -1) & (col <= FY)
            pnear = (prow >= -1) & (prow <= FX) & (pcol >= -1) & (pcol <= FY)
            ok = ok & (near | pnear)
        word = (row + H) * 128 + col + H + (((prow + H) * 128 + pcol + H) << 13)
        word = word + (mine << 26) + (theirs << 27) + (code << 28)
        word = jnp.where(ok, word, -1)
        for b in range(4):
            raw_v[4 * k + b : 4 * k + b + 1, :] = word[:, 128 * b : 128 * b + 128]
    copy = pltpu.make_async_copy(raw_v, raw_s, sems.at[20])
    copy.start()
    copy.wait()

    def scan_list(k, n):
        def scan(i, n):
            for j in range(8):
                at = i * 8 + j
                word = raw_s[k * 4 + (at >> 7), at & 127]
                words_s[n >> 7, n & 127] = word
                n = n + (word >= 0).astype(I32)
            return n

        return lax.fori_loop(0, (info_ref[4 + k] + 7) >> 3, scan, n)

    mine = scan_list(0, jnp.int32(0))
    total = lax.fori_loop(1, NLIST, scan_list, mine)

    def blank(i, carry):
        words_s[i >> 7, i & 127] = jnp.int32(-1)
        return carry

    lax.fori_loop(total, chunks(total + 1) * 128, blank, 0)
    count_out[0] = total
    count_out[1] = mine
    copy = pltpu.make_async_copy(words_s, words_out, sems.at[20])
    copy.start()
    for piece in copies:
        piece.wait()

    @pl.loop(0, chunks(total))
    def _(c):
        @pl.loop(0, 16)
        def _(i):
            for j in range(8):
                at = i * 8 + j
                word = jnp.maximum(words_s[c, at], 0)
                own = word & 8191
                other = (word >> 13) & 8191
                mine = (word >> 26) & 1
                theirs = (word >> 27) & 1
                orow, ocol = own >> 7, (own & 127) + PADC
                prow, pcol = other >> 7, (other & 127) + PADC
                stage[0, pl.ds(at, 1), :] = table[mine, orow, pl.ds(ocol, 1), :]
                stage[1, pl.ds(at, 1), :] = table[mine + 2, orow, pl.ds(ocol, 1), :]
                stage[2, pl.ds(at, 1), :] = table[theirs, prow, pl.ds(pcol, 1), :]
                stage[3, pl.ds(at, 1), :] = table[theirs + 2, prow, pl.ds(pcol, 1), :]

        for k in range(4):
            tiles[c, k] = jnp.transpose(stage[k]) * SC
        pltpu.make_async_copy(tiles.at[c], tiles_out.at[c], tile_sems.at[c]).start()

    copy.wait()
    split_ref[...] = jnp.zeros_like(split_ref)
    put_shift(split_ref, state_ref[0:1, :], state_ref[1:2, :])
    split16 = split_ref[...].astype(BF16)
    acc_ref[...] = jnp.zeros_like(acc_ref)

    @pl.loop(0, chunks(mine))
    def _(c):
        contact_chunk(c, mine, words_out, tiles, split16, hot_ref, b_ref, acc_ref)

    ax, ay = acc_rows(acc_ref)
    force_out[...] = jnp.zeros_like(force_out)
    force_out[0:1, :] = ax
    force_out[1:2, :] = ay

    @pl.loop(0, chunks(total))
    def _(c):
        pltpu.make_async_copy(tiles.at[c], tiles_out.at[c], tile_sems.at[c]).wait()


def later_kernel(
    count_ref, force_ref, state_ref, words_ref, tiles_in, vel_out, shift_out,
    tiles, hot_ref, b_ref, split_ref, acc_ref, now_ref, tile_sems,
):
    total = count_ref[0]

    @pl.loop(0, chunks(total))
    def _(c):
        pltpu.make_async_copy(tiles_in.at[c], tiles.at[c], tile_sems.at[c]).start()

    now_ref[...] = state_ref[...]

    def update(fx, fy):
        scale = DT / now_ref[4:5, :]
        vx = now_ref[2:3, :]
        vy = now_ref[3:4, :]
        vx = vx + (fx - DRAG * vx) * scale
        vy = vy + (fy - DRAG * vy) * scale
        now_ref[2:3, :] = vx
        now_ref[3:4, :] = vy
        now_ref[0:1, :] = now_ref[0:1, :] + DT * vx
        now_ref[1:2, :] = now_ref[1:2, :] + DT * vy

    update(force_ref[0:1, :], force_ref[1:2, :])
    split_ref[...] = jnp.zeros_like(split_ref)

    @pl.loop(0, chunks(total))
    def _(c):
        pltpu.make_async_copy(tiles_in.at[c], tiles.at[c], tile_sems.at[c]).wait()

    @pl.loop(1, STEPS)
    def _(step):
        put_shift(split_ref, now_ref[0:1, :], now_ref[1:2, :])
        split16 = split_ref[...].astype(BF16)
        acc_ref[...] = jnp.zeros_like(acc_ref)

        @pl.loop(0, chunks(total))
        def _(c):
            contact_chunk(c, total, words_ref, tiles, split16, hot_ref, b_ref, acc_ref)

        ax, ay = acc_rows(acc_ref)
        update(ax + force_ref[2:3, :], ay + force_ref[3:4, :])

    for out, base in ((shift_out, 0), (vel_out, 2)):
        for k in range(2):
            for r in range(FX):
                row = now_ref[base + k : base + k + 1, (r + H) * 128 : (r + H) * 128 + 128]
                out[r, k : k + 1, :] = pltpu.roll(row, 128 - H, 1)[:, 0:FY]


def moved(x, axis, up):
    count = lax.axis_size(axis)
    pairs = [(i, i + 1) if up else (i + 1, i) for i in range(count - 1)]
    return lax.ppermute(x, axis, pairs)


def as_rows(x, rows):
    flat = x.reshape(-1)
    return jnp.pad(flat, (0, rows * 512 - flat.shape[0])).reshape(rows, 512)


def shards(
    outline, centres, velocity, mass, response, pairs, pair_count, forcing, ocean_dest, ocean_floe
):
    rows_dev = forcing.shape[0]
    send = pl.pallas_call(
        send_kernel,
        out_shape=jax.ShapeDtypeStruct((DEVS * BLK, 128), F32),
        in_specs=[vspec()] * 3,
        out_specs=vspec(),
        scratch_shapes=[
            pltpu.VMEM((rows_dev // 128, 128), I32),
            pltpu.VMEM((DEVS, 128), F32),
            pltpu.SMEM((rows_dev // 128, 128), I32),
            pltpu.SemaphoreType.DMA,
        ],
        compiler_params=params(),
        cost_estimate=pl.CostEstimate(flops=100000000, bytes_accessed=4 << 20, transcendentals=0),
    )(ocean_dest.reshape(rows_dev // 128, 128), ocean_floe.reshape(rows_dev // 128, 128), forcing)
    got = lax.all_to_all(
        send.reshape(DEVS, BLK, 128), ("gx", "gy"), split_axis=0, concat_axis=0, tiled=True
    )

    state = jnp.concatenate(
        [jnp.transpose(centres, (2, 0, 1)), jnp.transpose(velocity, (2, 0, 1)), mass[None]], axis=0
    )
    lists = jnp.transpose(pairs[0, 0], (1, 0)).astype(F32)
    count = jnp.broadcast_to(pair_count.astype(F32), (1, 512))

    def pack_x(lo):
        return jnp.concatenate(
            [outline[lo : lo + H].reshape(H * FY, 512), as_rows(state[:, lo : lo + H], 2), lists, count,
             jnp.zeros((1, 512), F32)], axis=0
        )

    def unpack_x(got):
        return (
            got[: H * FY].reshape(H, FY, 512),
            got[H * FY : H * FY + 2].reshape(-1)[: 5 * H * FY].reshape(5, H, FY),
            got[H * FY + 2 : H * FY + 7],
        )

    north_o, north_s, north_l = unpack_x(moved(pack_x(FX - H), "gx", True))
    south_o, south_s, south_l = unpack_x(moved(pack_x(0), "gx", False))
    tall = jnp.concatenate([north_s, state, south_s], axis=1)
    own_l = jnp.concatenate([lists, count], axis=0)

    def pack_y(lo):
        cols = jnp.concatenate(
            [north_o[:, lo : lo + H], outline[:, lo : lo + H], south_o[:, lo : lo + H]], axis=0
        )
        return jnp.concatenate(
            [cols.reshape(R * H, 512), as_rows(tall[:, :, lo : lo + H], 1), north_l, own_l, south_l], axis=0
        )

    def unpack_y(got):
        return (
            got[: R * H].reshape(R, H, 512),
            got[R * H].reshape(-1)[: 5 * R * H].reshape(5, R, H),
            got[R * H + 1 : R * H + 16],
        )

    west_o, west_s, west_l = unpack_y(moved(pack_y(FY - H), "gy", True))
    east_o, east_s, east_l = unpack_y(moved(pack_y(0), "gy", False))
    west_o = jnp.pad(west_o, ((0, 0), (8 - H, 0), (0, 0)))
    east_o = jnp.pad(east_o, ((0, 0), (0, 8 - H), (0, 0)))
    wide = jnp.concatenate([west_s, tall, east_s], axis=2)
    wide = jnp.pad(wide, ((0, 0), (0, 0), (0, 128 - FY - 2 * H)))
    weight = jnp.where(wide[4:5] == 0.0, 1.0, wide[4:5])
    wide = jnp.concatenate([wide[:4], weight, jnp.zeros((3, R, 128), F32)], axis=0).reshape(8, NF)

    every = [own_l, north_l, south_l] + [
        block[5 * k : 5 * k + 5] for block in (west_l, east_l) for k in (0, 1, 2)
    ]
    lists36 = jnp.concatenate([block[:4] for block in every], axis=0)
    gx, gy = lax.axis_index("gx"), lax.axis_index("gy")
    info = jnp.concatenate(
        [
            jnp.stack([gx * FX, gy * FY, lax.axis_size("gx") * FX, lax.axis_size("gy") * FY]).astype(I32),
            jnp.stack([block[4, 0] for block in every]).astype(I32),
            jnp.zeros((3,), I32),
        ]
    )
    chunk_scratch = [
        pltpu.VMEM((NF, 128), BF16),
        pltpu.VMEM((3, 128, 128), F32),
        pltpu.VMEM((16, NF), F32),
        pltpu.VMEM((16, NF), F32),
    ]
    tiles, words, counts, contact = pl.pallas_call(
        first_kernel,
        out_shape=[
            jax.ShapeDtypeStruct((NCH, 4, 128, 128), F32),
            jax.ShapeDtypeStruct((NCH + 1, 128), I32),
            jax.ShapeDtypeStruct((2,), I32),
            jax.ShapeDtypeStruct((8, NF), F32),
        ],
        in_specs=[sspec(), vspec(), vspec()] + [aspec()] * 5,
        out_specs=[aspec(), vspec(), sspec(), vspec()],
        scratch_shapes=[
            pltpu.VMEM((4, R, TW, 128), F32),
            pltpu.VMEM((NCH, 4, 128, 128), F32),
            pltpu.VMEM((4, 128, 128), F32),
            pltpu.VMEM((NCH, 128), I32),
            pltpu.SMEM((NCH, 128), I32),
            pltpu.SMEM((NCH + 1, 128), I32),
            *chunk_scratch,
            pltpu.SemaphoreType.DMA((21,)),
            pltpu.SemaphoreType.DMA((NCH,)),
        ],
        compiler_params=params(),
        cost_estimate=pl.CostEstimate(flops=500000000, bytes_accessed=8 << 20, transcendentals=8 << 20),
    )(info, lists36, wide, outline, north_o, south_o, west_o, east_o)

    ocean = pl.pallas_call(
        ocean_kernel,
        out_shape=jax.ShapeDtypeStruct((8, NF), F32),
        in_specs=[vspec()] * 2,
        out_specs=vspec(),
        scratch_shapes=[
            pltpu.VMEM((FX * FY, 256), F32),
            pltpu.VMEM((3, DEVS * BLK // 384, 128), F32),
        ],
        compiler_params=params(),
        cost_estimate=pl.CostEstimate(flops=5000000000, bytes_accessed=5 << 20, transcendentals=0),
    )(got.reshape(DEVS * BLK, 128), response.reshape(FX * FY, NB))

    force = jnp.concatenate([contact[:2] + ocean[:2], ocean[:2]], axis=0).reshape(4, R, 128)
    w = 2 * H - 1
    low, high = moved(force[:, FX : FX + w], "gx", True), moved(force[:, 1 : 1 + w], "gx", False)
    force = force + jnp.pad(low, ((0, 0), (0, R - w), (0, 0))) + jnp.pad(high, ((0, 0), (R - w, 0), (0, 0)))
    low, high = moved(force[:, :, FY : FY + w], "gy", True), moved(force[:, :, 1 : 1 + w], "gy", False)
    c = FY + 2 * H
    force = force + jnp.pad(low, ((0, 0), (0, 0), (0, 128 - w))) + jnp.pad(high, ((0, 0), (0, 0), (c - w, 128 - c)))
    force = jnp.pad(force.reshape(4, NF), ((0, 4), (0, 0)))

    vel, shift = pl.pallas_call(
        later_kernel,
        out_shape=[jax.ShapeDtypeStruct((FX, 2, FY), F32)] * 2,
        in_specs=[sspec(), vspec(), vspec(), vspec(), aspec()],
        out_specs=[vspec()] * 2,
        scratch_shapes=[
            pltpu.VMEM((NCH, 4, 128, 128), F32),
            *chunk_scratch,
            pltpu.VMEM((8, NF), F32),
            pltpu.SemaphoreType.DMA((NCH,)),
        ],
        compiler_params=params(),
        cost_estimate=pl.CostEstimate(flops=500000000, bytes_accessed=4 << 20, transcendentals=16 << 20),
    )(counts, force, wide, words, tiles)
    return jnp.transpose(vel, (0, 2, 1)), jnp.transpose(shift, (0, 2, 1))


def solution(mesh):
    return jax.shard_map(
        shards,
        mesh=mesh,
        in_specs=(
            P("gx", "gy", None),
            P("gx", "gy", None),
            P("gx", "gy", None),
            P("gx", "gy"),
            P("gx", "gy", None),
            P("gx", "gy", None, None),
            P("gx", "gy"),
            P(("gx", "gy"), None),
            P(("gx", "gy"), None),
            P(("gx", "gy")),
        ),
        out_specs=(P("gx", "gy", None), P("gx", "gy", None)),
        check_vma=False,
    )
```

time: 527 us -> 195 us (0.37)
  the two profiles are of different devices: /device:TPU:33 before, /device:TPU:62 now
where the time goes in v1:
time: 195 us; the launch traced here: 197 us
  Pallas kernels  112 us (57%)
  starting transfers between devices  32.7 us (17%)
  waiting for transfers between devices  32.5 us (17%)
  local copies, waits for them, and re-layouts  15.9 us (8%)
  other arithmetic  2.23 us (1%)
    pallas_call x1, Pallas kernels, shards(): pl.pallas_call(later_kernel, out_shape=[jax.ShapeDtypeStruct((FX, 2, FY),...  46.3 us
    pallas_call x1, Pallas kernels, shards(): pl.pallas_call(first_kernel, out_shape=[jax.ShapeDtypeStruct((NCH, 4, 128...  38.5 us
    ppermute x8, waiting for transfers between devices, moved(): return lax.ppermute(x, axis, pairs)  32.5 us
    ppermute x8, starting transfers between devices, moved(): return lax.ppermute(x, axis, pairs)  21.6 us
    pallas_call x1, Pallas kernels, shards(): pl.pallas_call(ocean_kernel, out_shape=jax.ShapeDtypeStruct((8, NF), F32)...  16.2 us
    all_to_all x1, starting transfers between devices, shards(): lax.all_to_all(send.reshape(DEVS, BLK, 128), ('gx', 'gy'), split_axis=0,...  11.1 us
    pallas_call x1, Pallas kernels, shards(): pl.pallas_call(send_kernel, out_shape=jax.ShapeDtypeStruct((DEVS * BLK, 1...  11.1 us
    another operation x1, local copies, waits for them, and re-layouts, shards(): jnp.stack([block[4, 0] for block in every]).astype(I32)  5.06 us
  transfers between devices with their start and end apart: 9, of which 5 were waited for; matrix products, arithmetic and copies ran while one was open for 6% of the time, Pallas kernels for 25%

profile of v1, /device:TPU:62, one launch (start us, length us, event | category | flops | bytes accessed | tf_op | source)
XLA Modules:
  0.0 197.3 jit_solution(12948210921992081318)
XLA Ops:
  1.3 0.7 convert_bitcast_fusion
  2.0 0.8 pad_maximum_fusion.4
  2.9 1.1 fusion.10
  4.0 2.1 %collective-permute-start.1 = (f32[136,512]{1,0:T(8,128)S(1)}, f32[136,512]{1,0:T(8,128)S(1)}, u32[]{:S(2)}, u32[]{:S(2)}) collective-permute-start(f32[136,512]{1,0:T(8,128)S(1)} %concatenate.44), channel_id=1, source_target_pairs={{16,0},{32,16},{48,32},{64,48},{80,64},{96,80},{112,96},{17,1},{33... | collective-permute-start | bytes 835592 | tf_op jit(solution)/shard_map/ppermute | solution.py:413
  6.3 2.2 %collective-permute-start = (f32[136,512]{1,0:T(8,128)S(1)}, f32[136,512]{1,0:T(8,128)S(1)}, u32[]{:S(2)}, u32[]{:S(2)}) collective-permute-start(f32[136,512]{1,0:T(8,128)S(1)} %concatenate.43), channel_id=1, source_target_pairs={{0,16},{16,32},{32,48},{48,64},{64,80},{80,96},{96,112},{1,17},{17... | collective-permute-start | bytes 835592 | tf_op jit(solution)/shard_map/ppermute | solution.py:413
  8.5 1.2 copy-done
  11.1 11.1 %shard_map.114 = f32[6144,128]{1,0:T(8,128)} custom-call(s32[16,128]{1,0:T(8,128)S(1)} %bitcast.45, s32[16,128]{1,0:T(8,128)S(1)} %bitcast.46, f32[2048,128]{1,0:T(8,128)S(1)} %copy-done), custom_call_target="tpu_custom_call" | custom-call | flops 100000000 | bytes 4194304 | tf_op jit(solution)/shard_map/pallas_call | solution.py:425
  22.3 11.1 %all-to-all-start = ((f32[128,48,128]{2,1,0:T(8,128)}), f32[128,48,128]{2,1,0:T(8,128)}, u32[]{:S(2)}, u32[]{:S(2)}) async-start(f32[128,48,128]{2,1,0:T(8,128)} %bitcast.48), calls=%async_computation | async-start | bytes 6291456 | tf_op jit(solution)/shard_map/all_to_all | solution.py:439
  33.4 1.3 fusion.9
  35.9 3.6 %collective-permute-start.2 = (f32[88,512]{1,0:T(8,128)S(1)}, f32[88,512]{1,0:T(8,128)S(1)}, u32[]{:S(2)}, u32[]{:S(2)}) collective-permute-start(f32[88,512]{1,0:T(8,128)S(1)} %concatenate.47), channel_id=1, source_target_pairs={{0,1},{1,2},{2,3},{3,4},{4,5},{5,6},{6,7},{7,8},{8,9},{9,10},{10,1... | collective-permute-start | bytes 540680 | tf_op jit(solution)/shard_map/ppermute | solution.py:413
  40.0 2.2 %collective-permute-start.3 = (f32[88,512]{1,0:T(8,128)S(1)}, f32[88,512]{1,0:T(8,128)S(1)}, u32[]{:S(2)}, u32[]{:S(2)}) collective-permute-start(f32[88,512]{1,0:T(8,128)S(1)} %concatenate.49), channel_id=1, source_target_pairs={{1,0},{2,1},{3,2},{4,3},{5,4},{6,5},{7,6},{8,7},{9,8},{10,9},{11,1... | collective-permute-start | bytes 540680 | tf_op jit(solution)/shard_map/ppermute | solution.py:413
  43.4 27.9 %collective-permute-done.2 = f32[88,512]{1,0:T(8,128)S(1)} collective-permute-done((f32[88,512]{1,0:T(8,128)S(1)}, f32[88,512]{1,0:T(8,128)S(1)}, u32[]{:S(2)}, u32[]{:S(2)}) %collective-permute-start.2) | collective-permute-done | bytes 180256 | tf_op jit(solution)/shard_map/ppermute | solution.py:413
  72.2 0.8 collective-permute-done.3
  73.7 5.1 %stack.11 = f32[9]{0:T(128)S(1)} concatenate(f32[1]{0:T(128)} %bitcast.2, f32[1]{0:T(128)} %bitcast.11, f32[1]{0:T(128)} %bitcast.14, f32[1]{0:T(128)} %bitcast.18, f32[1]{0:T(128)} %bitcast.19, f32[1]{0:T(128)} %bitcast.20, f32[1]{0:T(128)} %bitcast.22, f32[1]{0:T(128)} %bitcast.23, f32[1]{0:T(128)} %bitcast.24), dimensions={0} | concatenate | bytes 72 | tf_op jit(solution)/shard_map/stack | solution.py:499
  79.3 0.9 pad.52.east_ref
  80.6 38.5 %shard_map.113 = (f32[36,4,128,128]{3,2,1,0:T(8,128)}, s32[37,128]{1,0:T(8,128)S(1)}, s32[2]{0:T(128)S(1)}, f32[8,4608]{1,0:T(8,128)S(1)}) custom-call(s32[16]{0:T(128)S(1)} %concatenate.50.info_ref, f32[36,512]{1,0:T(8,128)S(1)} %concatenate.51.lists_ref, f32[8,4608]{1,0:T(8,128)S(1)} %maximum_bitcast_fusion.state_ref, f32[32,64,512]{2,1,0:T(8,128)} %outline_ref.1, ...), custom_call_target="tpu_custom_call" | custom-call | flops 500000000 | bytes 8388608 | tf_op jit(solution)/shard_map/pallas_call | solution.py:509
  119.2 16.2 %shard_map.115 = f32[8,4608]{1,0:T(8,128)S(1)} custom-call(f32[6144,128]{1,0:T(8,128)} %bitcast.29.rows_ref, f32[2048,64]{1,0:T(8,128)S(1)} %bitcast.47), custom_call_target="tpu_custom_call" | custom-call | flops 5000000000 | bytes 5242880 | tf_op jit(solution)/shard_map/pallas_call | solution.py:534
  135.6 1.9 collective-permute-start.4
  137.5 3.6 %collective-permute-start.5 = (f32[4,3,128]{2,1,0:T(4,128)S(1)}, f32[4,3,128]{2,1,0:T(4,128)S(1)}, u32[]{:S(2)}, u32[]{:S(2)}) collective-permute-start(f32[4,3,128]{2,1,0:T(4,128)S(1)} %get-tuple-element.41), channel_id=1, source_target_pairs={{16,0},{32,16},{48,32},{64,48},{80,64},{96,80},{112,96},{17,1},{33... | collective-permute-start | bytes 18440 | tf_op jit(solution)/shard_map/ppermute | solution.py:413
  141.1 1.3 collective-permute-done.5
  142.6 1.9 collective-permute-start.6
  144.5 3.9 %collective-permute-start.7 = (f32[4,36,3]{2,1,0:T(8,128)S(1)}, f32[4,36,3]{2,1,0:T(8,128)S(1)}, u32[]{:S(2)}, u32[]{:S(2)}) collective-permute-start(f32[4,36,3]{2,1,0:T(8,128)S(1)} %get-tuple-element.39), channel_id=1, source_target_pairs={{1,0},{2,1},{3,2},{4,3},{5,4},{6,5},{7,6},{8,7},{9,8},{10,9},{11,1... | collective-permute-start | bytes 5192 | tf_op jit(solution)/shard_map/ppermute | solution.py:413
  148.9 1.9 collective-permute-done.7
  151.0 46.3 %shard_map.116 = (f32[32,2,64]{2,1,0:T(2,128)}, f32[32,2,64]{2,1,0:T(2,128)}) custom-call(s32[2]{0:T(128)S(1)} %get-tuple-element.8.count_ref, f32[8,4608]{1,0:T(8,128)S(1)} %pad.57.force_ref, f32[8,4608]{1,0:T(8,128)S(1)} %maximum_bitcast_fusion.state_ref, s32[37,128]{1,0:T(8,128)S(1)} %get-tuple-element.10.words_ref, ...), custom_call_target="tpu_custom_call" | custom-call | flops 500000000 | bytes 4194304 | tf_op jit(solution)/shard_map/pallas_call | solution.py:556
  (95 shorter events, 7.6 us)
Async XLA Ops:
  4.0 30.7 %collective-permute-start.1 = (f32[136,512]{1,0:T(8,128)S(1)}, f32[136,512]{1,0:T(8,128)S(1)}, u32[]{:S(2)}, u32[]{:S(2)}) collective-permute-start(f32[136,512]{1,0:T(8,128)S(1)} %concatenate.44), channel_id=1, source_target_pairs={{16,0},{32,16},{48,32},{64,48},{80,64},{96,80},{112,96},{17,1},{33... | collective-permute-start | bytes 835592 | tf_op jit(solution)/shard_map/ppermute | solution.py:413
  6.3 28.5 %collective-permute-start = (f32[136,512]{1,0:T(8,128)S(1)}, f32[136,512]{1,0:T(8,128)S(1)}, u32[]{:S(2)}, u32[]{:S(2)}) collective-permute-start(f32[136,512]{1,0:T(8,128)S(1)} %concatenate.43), channel_id=1, source_target_pairs={{0,16},{16,32},{32,48},{48,64},{64,80},{80,96},{96,112},{1,17},{17... | collective-permute-start | bytes 835592 | tf_op jit(solution)/shard_map/ppermute | solution.py:413
  8.5 1.2 copy-start
  9.7 0.7 copy-start.1
  10.4 0.7 copy-start.2
  22.3 13.1 %copy-start.4 = (f32[32,64,2]{1,2,0:T(2,128)S(1)}, f32[32,64,2]{1,2,0:T(2,128)}, u32[]{:S(2)}) copy-start(f32[32,64,2]{1,2,0:T(2,128)} %param.12) | copy-start | bytes 49156
  22.3 13.1 %copy-start.5 = (f32[32,64,2]{1,2,0:T(2,128)S(1)}, f32[32,64,2]{1,2,0:T(2,128)}, u32[]{:S(2)}) copy-start(f32[32,64,2]{1,2,0:T(2,128)} %param.11) | copy-start | bytes 49156
  22.3 13.1 %copy-start.6 = (f32[32,64]{1,0:T(8,128)S(1)}, f32[32,64]{1,0:T(8,128)}, u32[]{:S(2)}) copy-start(f32[32,64]{1,0:T(8,128)} %param.13) | copy-start | bytes 24580
  22.3 96.8 %all-to-all-start = ((f32[128,48,128]{2,1,0:T(8,128)}), f32[128,48,128]{2,1,0:T(8,128)}, u32[]{:S(2)}, u32[]{:S(2)}) async-start(f32[128,48,128]{2,1,0:T(8,128)} %bitcast.48), calls=%async_computation | async-start | bytes 6291456 | tf_op jit(solution)/shard_map/all_to_all | solution.py:439
  35.9 35.5 %collective-permute-start.2 = (f32[88,512]{1,0:T(8,128)S(1)}, f32[88,512]{1,0:T(8,128)S(1)}, u32[]{:S(2)}, u32[]{:S(2)}) collective-permute-start(f32[88,512]{1,0:T(8,128)S(1)} %concatenate.47), channel_id=1, source_target_pairs={{0,1},{1,2},{2,3},{3,4},{4,5},{5,6},{6,7},{7,8},{8,9},{9,10},{10,1... | collective-permute-start | bytes 540680 | tf_op jit(solution)/shard_map/ppermute | solution.py:413
  40.0 33.0 %collective-permute-start.3 = (f32[88,512]{1,0:T(8,128)S(1)}, f32[88,512]{1,0:T(8,128)S(1)}, u32[]{:S(2)}, u32[]{:S(2)}) collective-permute-start(f32[88,512]{1,0:T(8,128)S(1)} %concatenate.49), channel_id=1, source_target_pairs={{1,0},{2,1},{3,2},{4,3},{5,4},{6,5},{7,6},{8,7},{9,8},{10,9},{11,1... | collective-permute-start | bytes 540680 | tf_op jit(solution)/shard_map/ppermute | solution.py:413
  80.6 38.5 %copy-start.3 = (f32[32,64,64]{2,1,0:T(8,128)S(1)}, f32[32,64,64]{2,1,0:T(8,128)}, u32[]{:S(2)}) copy-start(f32[32,64,64]{2,1,0:T(8,128)} %param.14) | copy-start | bytes 1572868
  135.6 5.6 %collective-permute-start.4 = (f32[4,3,128]{2,1,0:T(4,128)S(1)}, f32[4,3,128]{2,1,0:T(4,128)S(1)}, u32[]{:S(2)}, u32[]{:S(2)}) collective-permute-start(f32[4,3,128]{2,1,0:T(4,128)S(1)} %get-tuple-element.40), channel_id=1, source_target_pairs={{0,16},{16,32},{32,48},{48,64},{64,80},{80,96},{96,112},{1,17},{17... | collective-permute-start | bytes 18440 | tf_op jit(solution)/shard_map/ppermute | solution.py:413
  137.5 5.0 %collective-permute-start.5 = (f32[4,3,128]{2,1,0:T(4,128)S(1)}, f32[4,3,128]{2,1,0:T(4,128)S(1)}, u32[]{:S(2)}, u32[]{:S(2)}) collective-permute-start(f32[4,3,128]{2,1,0:T(4,128)S(1)} %get-tuple-element.41), channel_id=1, source_target_pairs={{16,0},{32,16},{48,32},{64,48},{80,64},{96,80},{112,96},{17,1},{33... | collective-permute-start | bytes 18440 | tf_op jit(solution)/shard_map/ppermute | solution.py:413
  142.6 6.3 %collective-permute-start.6 = (f32[4,36,3]{2,1,0:T(8,128)S(1)}, f32[4,36,3]{2,1,0:T(8,128)S(1)}, u32[]{:S(2)}, u32[]{:S(2)}) collective-permute-start(f32[4,36,3]{2,1,0:T(8,128)S(1)} %get-tuple-element.38), channel_id=1, source_target_pairs={{0,1},{1,2},{2,3},{3,4},{4,5},{5,6},{6,7},{7,8},{8,9},{9,10},{10,1... | collective-permute-start | bytes 5192 | tf_op jit(solution)/shard_map/ppermute | solution.py:413
  144.5 6.3 %collective-permute-start.7 = (f32[4,36,3]{2,1,0:T(8,128)S(1)}, f32[4,36,3]{2,1,0:T(8,128)S(1)}, u32[]{:S(2)}, u32[]{:S(2)}) collective-permute-start(f32[4,36,3]{2,1,0:T(8,128)S(1)} %get-tuple-element.39), channel_id=1, source_target_pairs={{1,0},{2,1},{3,2},{4,3},{5,4},{6,5},{7,6},{8,7},{9,8},{10,9},{11,1... | collective-permute-start | bytes 5192 | tf_op jit(solution)/shard_map/ppermute | solution.py:413
